TPU v7x, 32 devices: a whole 2x2x4 slice. The times are simulated.
32 devices in a mesh: region: 8 (over z, x), level: 4 (over y, core).
Axes of the slice: x: 2, y: 2, z: 4, core: 2. Of those that a mesh axis runs over, the one named last changes fastest.
Arguments:
- ensemble: bfloat16 [4, 256, 32768], P('level', None, 'region'), may hold values from -6 to 6
- obs_anomaly: bfloat16 [4, 8192, 256], P('level', 'region'), may hold values from -6 to 6
- innovation: bfloat16 [4, 8192], P('level', 'region'), may hold values from -18 to 18
- obs_precision: bfloat16 [4, 8192], P('level', 'region'), may hold values from 0.019897461 to 0.29882812
- owner_region: int32 [4, 8192, 1], P('level', 'region'), may hold values from 0 to 7; in each aligned block of 1024 rows (0 to 1023, 1024 to 2047, ..., all dimensions but the last counted through in order) at most 192 rows name the same one
- neighbours: int32 [8, 3], replicated, may hold values from 0 to 7, all different within a row
Outputs:
- analysis: bfloat16 [4, 256, 32768], P('level', None, 'region')
Inputs may be any that keep to these rules, and one draw needn't show every extreme that they name: `owner_region`: among the 1024 observations of one device (aligned blocks), no region is named more than 192 times, a bound that some block reaches. `neighbours`: each row lists 3 different regions; every region is listed by some row.
All inputs are finite; a program needn't handle non-finite values.
Results may differ from a plain program's by a relative error of at most 0.0059.
Values may be sent and summed in bfloat16 or wider, within the bound.
A program may use at most 64 MiB of HBM per device.

v0:
```python
import math

import jax
import jax.numpy as jnp
from jax import lax
from jax.sharding import PartitionSpec as P

NSTEPS = 4


TAPER = 0.6


def neighbour_weights(neighbours):
    region_ids = jnp.arange(neighbours.shape[0], dtype=jnp.int32)
    weights = (region_ids[:, None] == region_ids[None, :]).astype(jnp.float32)
    for listed in range(neighbours.shape[1]):
        hit = (neighbours[:, listed][:, None] == region_ids[None, :]).astype(jnp.float32)
        weights = weights + TAPER ** (listed + 1) * hit
    return weights


def inverse_root(matrix):
    order_size = matrix.shape[0]
    identity = jnp.eye(order_size, dtype=jnp.float32)
    norm_scale = 0.5 * jnp.sqrt(jnp.sum(matrix * matrix))
    root_iter = matrix / norm_scale
    inverse_iter = identity
    for newton_step in range(NSTEPS):
        correction = 1.5 * identity - 0.5 * jnp.dot(
            inverse_iter, root_iter, precision=lax.Precision.HIGHEST
        )
        root_iter = jnp.dot(root_iter, correction, precision=lax.Precision.HIGHEST)
        inverse_iter = jnp.dot(correction, inverse_iter, precision=lax.Precision.HIGHEST)
    return inverse_iter / jnp.sqrt(norm_scale)


def analysis_weights(covariance, innovation_sum):
    order_size = covariance.shape[0]
    identity = jnp.eye(order_size, dtype=jnp.float32)
    precision_matrix = covariance + (order_size - 1.0) * identity
    root = inverse_root(precision_matrix)
    inner = jnp.dot(root, innovation_sum, precision=lax.Precision.HIGHEST)
    mean_shift = jnp.dot(root, inner, precision=lax.Precision.HIGHEST)
    return (math.sqrt(order_size - 1.0) * root + mean_shift[:, None]).astype(jnp.bfloat16)


def update_columns(column_block, transform):
    average = jnp.mean(column_block.astype(jnp.float32), axis=0)
    anomaly = (column_block.astype(jnp.float32) - average[None, :]).astype(jnp.bfloat16)
    combined = lax.dot_general(
        transform, anomaly, (((0,), (0,)), ((), ())), preferred_element_type=jnp.float32
    )
    return (combined + average[None, :]).astype(jnp.bfloat16)


def level_factor(distance, levels):
    factor = jnp.zeros(distance.shape, jnp.float32)
    for apart in range(levels):
        factor = factor + 0.5**apart * (distance == apart).astype(jnp.float32)
    return factor


def body(ensemble, obs_anomaly, innovation, obs_precision, owner_region, neighbours):
    regions = lax.axis_size("region")
    levels = lax.axis_size("level")
    my_level = lax.axis_index("level")
    members = obs_anomaly.shape[2]
    local_obs = obs_anomaly.shape[1]
    capacity = 3 * local_obs // (2 * regions)
    slot_count = (neighbours.shape[1] + 1) * capacity
    region_weight = neighbour_weights(neighbours)
    owner_ids = owner_region[0, :, 0]
    region_ids = jnp.arange(regions, dtype=jnp.int32)
    owner_table = (owner_ids[:, None] == region_ids[None, :]).astype(jnp.float32)
    dest_weight = jnp.dot(owner_table, region_weight.T, precision=lax.Precision.HIGHEST)
    live = dest_weight > 0
    position = jnp.cumsum(live.astype(jnp.int32), axis=0) - 1
    gain = (dest_weight * obs_precision[0].astype(jnp.float32)[:, None]).astype(jnp.bfloat16)
    slot_ids = jnp.arange(slot_count, dtype=jnp.int32)
    placement = jnp.logical_and(
        live.T[:, None, :], position.T[:, None, :] == slot_ids[None, :, None]
    )
    place_float = placement.astype(jnp.float32)
    send_rows = jnp.einsum(
        "rso,om->rsm",
        placement.astype(jnp.bfloat16),
        obs_anomaly[0],
        preferred_element_type=jnp.float32,
    ).astype(jnp.bfloat16)
    send_gain = jnp.einsum(
        "rso,or->rs", place_float, gain.astype(jnp.float32), precision=lax.Precision.HIGHEST
    ).astype(jnp.bfloat16)
    send_innov = jnp.einsum(
        "rso,o->rs", place_float, innovation[0].astype(jnp.float32), precision=lax.Precision.HIGHEST
    ).astype(jnp.bfloat16)
    received = (
        lax.all_to_all(send_rows, "region", split_axis=0, concat_axis=0, tiled=True),
        lax.all_to_all(send_gain, "region", split_axis=0, concat_axis=0, tiled=True),
        lax.all_to_all(send_innov, "region", split_axis=0, concat_axis=0, tiled=True),
    )
    routed_rows = received[0].reshape(-1, members)
    routed_gain = received[1].reshape(-1)
    routed_innov = received[2].reshape(-1)
    weighted = (routed_gain.astype(jnp.float32)[:, None] * routed_rows.astype(jnp.float32)).astype(
        jnp.bfloat16
    )
    own_cov = jnp.dot(weighted.T, routed_rows, preferred_element_type=jnp.float32)
    own_sum = jnp.dot(routed_innov, weighted, preferred_element_type=jnp.float32)
    stacked = jnp.tile(own_cov, (levels, 1))
    target_level = jnp.arange(members * lax.axis_size("level"), dtype=jnp.int32) // members
    factor = level_factor(jnp.abs(target_level - my_level), levels)
    covariance = lax.psum_scatter(
        factor[:, None] * stacked, "level", scatter_dimension=0, tiled=True
    )
    level_ids = jnp.arange(levels, dtype=jnp.int32)
    sum_terms = level_factor(jnp.abs(level_ids - my_level), levels)[:, None] * own_sum[None, :]
    all_sums = lax.psum(sum_terms, "level")
    innovation_sum = lax.dynamic_index_in_dim(all_sums, my_level, 0, keepdims=False)
    transform = analysis_weights(covariance, innovation_sum)
    return update_columns(ensemble[0], transform)[None]


def solution(mesh):
    return jax.shard_map(
        body,
        mesh=mesh,
        in_specs=(
            P("level", None, "region"),
            P("level", "region", None),
            P("level", "region"),
            P("level", "region"),
            P("level", "region", None),
            P(),
        ),
        out_specs=P("level", None, "region"),
        check_vma=False,
    )
```

profile of v0, /device:TPU:0, one launch (start us, length us, event | category | flops | bytes accessed | tf_op | source)
XLA Modules:
  0.0 158.2 jit_solution(9394405093534937357)
XLA Ops:
  6.5 0.0 copy-start
  6.5 0.8 slice_bitcast_fusion.2
  7.3 1.1 fusion.32
  8.5 2.3 %reduce-window.6 = s32[8,8,128]{2,1,0:T(8,128)S(1)} reduce-window(s32[8,8,128]{2,1,0:T(8,128)S(1)} %copy.13, s32[]{:T(128)} %constant.35.clone.1), window={size=1x1x128 pad=0_0x0_0x127_0}, to_apply=%region_0.0 | reduce-window | flops 1040384 | bytes 65540 | tf_op jit(solution)/shard_map/reduce-window
  10.8 0.3 slice_reduce_fusion
  11.1 0.2 reduce-window.9
  11.2 0.1 add_bitcast_fusion
  11.3 0.7 convert_element_type.111
  12.0 5.2 %fusion.5 = bf16[8,1,768]{2,1,0:T(2,128)(2,1)S(1)} fusion(s32[8,1024]{1,0:T(8,128)S(1)} %bitcast.95, pred[8,1024]{1,0:T(8,128)(4,1)S(1)} %get-tuple-element.6, bf16[1024,8,1]{0,1,2:T(8,128)(2,1)S(1)} %fusion.43), kind=kOutput, calls=%fused_computation.4 | convolution fusion | flops 25165824 | bytes 69632 | tf_op jit(solution)/shard_map/rso,or->rs/dot_general | solution.py:91
  17.3 0.5 broadcast.244
  17.8 0.6 reduce.3
  18.4 0.6 reshape.122
  19.0 7.3 %all-to-all-start = ((bf16[8,2,384]{2,1,0:T(2,128)(2,1)}), bf16[8,2,384]{2,1,0:T(2,128)(2,1)S(1)}, u32[]{:S(2)}, u32[]{:S(2)}) async-start(bf16[8,2,384]{2,1,0:T(2,128)(2,1)} %reshape.122), calls=%async_computation | async-start | bytes 24576 | tf_op jit(solution)/shard_map/all_to_all | solution.py:99
  26.2 0.0 copy-done
  26.2 6.7 %fusion.21 = bf16[8,768,256]{2,1,0:T(8,128)(2,1)} fusion(s32[8,1024]{1,0:T(8,128)S(1)} %bitcast.96, pred[8,1024]{1,0:T(8,128)(4,1)S(1)} %get-tuple-element.6, bf16[1,1024,256]{2,1,0:T(8,128)(2,1)S(1)} %copy-done), kind=kOutput, calls=%fused_computation.23 | convolution fusion | flops 3235381248 | bytes 3710976 | tf_op jit(solution)/shard_map/rso,om->rsm/dot_general | solution.py:85
  32.9 0.0 all-to-all-done
  32.9 6.0 %all-to-all-start.1 = ((bf16[8,768,256]{2,1,0:T(8,128)(2,1)}), bf16[8,768,256]{2,1,0:T(8,128)(2,1)}, u32[]{:S(2)}, u32[]{:S(2)}) async-start(bf16[8,768,256]{2,1,0:T(8,128)(2,1)} %fusion.21), calls=%async_computation.1 | async-start | bytes 6291456 | tf_op jit(solution)/shard_map/all_to_all | solution.py:98
  38.9 0.2 reduce-scatter.2.cloned.1.call-start
  39.2 70.0 %all-to-all-done.1 = bf16[8,768,256]{2,1,0:T(8,128)(2,1)} async-done(((bf16[8,768,256]{2,1,0:T(8,128)(2,1)}), bf16[8,768,256]{2,1,0:T(8,128)(2,1)}, u32[]{:S(2)}, u32[]{:S(2)}) %all-to-all-start.1) | async-done | bytes 3145760 | tf_op jit(solution)/shard_map/all_to_all | solution.py:98
  109.2 0.0 copy-start.2
  109.2 4.8 %fusion.30 = f32[256,256]{1,0:T(8,128)S(1)} fusion(bf16[8,768,256]{2,1,0:T(8,128)(2,1)} %all-to-all-done.1, f32[8,768]{1,0:T(8,128)S(1)} %bitcast.98), kind=kOutput, calls=%fused_computation.34 | convolution fusion | flops 810024960 | bytes 3432448 | tf_op jit(solution)/shard_map/dot_general | solution.py:108
  114.0 1.2 bitcast_multiply_fusion
  115.1 0.0 reduce-scatter.2.cloned.1.call-update
  115.2 0.0 copy-done.2
  115.2 0.0 copy-start.1
  115.2 5.2 %fusion.1 = bf16[1,8,768]{2,0,1:T(2,128)(2,1)S(1)} fusion(s32[8,1024]{1,0:T(8,128)S(1)} %bitcast.97, pred[8,1024]{1,0:T(8,128)(4,1)S(1)} %get-tuple-element.6, bf16[1,1024]{1,0:T(2,128)(2,1)S(1)} %copy-done.2), kind=kOutput, calls=%fused_computation.2 | convolution fusion | flops 25165824 | bytes 55296 | tf_op jit(solution)/shard_map/rso,o->rs/dot_general | solution.py:94
  120.4 0.6 reduce.4
  121.0 0.6 reshape.124
  121.6 3.6 %all-to-all-start.2 = ((bf16[8,2,384]{2,1,0:T(2,128)(2,1)}), bf16[8,2,384]{2,1,0:T(2,128)(2,1)S(1)}, u32[]{:S(2)}, u32[]{:S(2)}) async-start(bf16[8,2,384]{2,1,0:T(2,128)(2,1)} %reshape.124), calls=%async_computation.3 | async-start | bytes 24576 | tf_op jit(solution)/shard_map/all_to_all | solution.py:100
  125.2 0.0 copy-done.1
  125.2 0.3 convert_reduce_fusion
  125.6 6.2 %all-to-all-done.2 = bf16[8,2,384]{2,1,0:T(2,128)(2,1)S(1)} async-done(((bf16[8,2,384]{2,1,0:T(2,128)(2,1)}), bf16[8,2,384]{2,1,0:T(2,128)(2,1)S(1)}, u32[]{:S(2)}, u32[]{:S(2)}) %all-to-all-start.2) | async-done | bytes 12320 | tf_op jit(solution)/shard_map/all_to_all | solution.py:100
  131.8 2.6 %fusion.15 = f32[1,256,1]{1,0,2:T(1,128)S(1)} fusion(bf16[8,768,256]{2,1,0:T(8,128)(2,1)} %all-to-all-done.1, f32[8,768]{1,0:T(8,128)S(1)} %bitcast.99, bf16[8,1,768]{2,1,0:T(2,128)(2,1)S(1)} %reshape.125), kind=kOutput, calls=%fused_computation.17 | convolution fusion | flops 7864320 | bytes 3183616 | tf_op jit(solution)/shard_map/dot_general | solution.py:109
  134.4 0.1 broadcast_multiply_fusion.1
  134.5 5.6 %psum.7 = f32[4,256]{1,0:T(4,128)S(1)} all-reduce(f32[4,256]{1,0:T(4,128)S(1)} %broadcast_multiply_fusion.1), channel_id=1, replica_groups=mesh['region'=8,'level'=4] {'level'}, use_global_device_ids=true, to_apply=%region_4.5 | all-reduce | flops 1024 | bytes 8192 | tf_op jit(solution)/shard_map/psum | solution.py:118
  140.1 0.0 reduce-scatter.2.cloned.1.call-done
  140.1 1.6 %multiply_reduce_fusion = f32[]{:T(128)} fusion(f32[256,256]{1,0:T(8,128)} %reduce-scatter.2.cloned.1.call-done), kind=kLoop, calls=%fused_computation.41 | loop fusion | flops 327679 | bytes 262148 | tf_op jit(solution)/shard_map/reduce_sum | solution.py:26
  142.5 1.3 fusion.29
  143.8 0.3 fusion.34
  144.0 1.4 fusion.38
  145.4 0.4 fusion.28
  145.8 0.4 fusion.86
  146.2 0.4 fusion.85
  146.6 0.4 fusion.27
  146.9 0.4 fusion.88
  147.3 0.4 fusion.87
  147.8 0.4 fusion.26
  148.2 0.4 convolution_divide_fusion
  148.5 0.3 convolution_bitcast_fusion
  148.8 0.3 fusion.89
  149.1 2.2 %fusion.14 = bf16[1,256,4096]{2,1,0:T(8,128)(2,1)} fusion(bf16[1,256,4096]{2,1,0:T(8,128)(2,1)S(1)} %copy-done.1, f32[4096]{0:T(1024)S(1)} %broadcast_multiply_fusion, f32[256,256]{1,0:T(8,128)S(1)} %convolution_divide_fusion, f32[256]{0:T(256)S(1)} %bitcast.102), kind=kOutput, calls=%fused_computation.16 | convolution fusion | flops 542310400 | bytes 4473856 | tf_op jit(solution)/shard_map/dot_general | solution.py:51
  (12 shorter events, 0.1 us)
Async XLA Ops:
  6.5 19.7 %copy-start = (bf16[1,1024,256]{2,1,0:T(8,128)(2,1)S(1)}, bf16[1,1024,256]{2,1,0:T(8,128)(2,1)}, u32[]{:S(2)}) copy-start(bf16[1,1024,256]{2,1,0:T(8,128)(2,1)} %param.7) | copy-start | bytes 1572868
  19.0 14.0 %all-to-all-start = ((bf16[8,2,384]{2,1,0:T(2,128)(2,1)}), bf16[8,2,384]{2,1,0:T(2,128)(2,1)S(1)}, u32[]{:S(2)}, u32[]{:S(2)}) async-start(bf16[8,2,384]{2,1,0:T(2,128)(2,1)} %reshape.122), calls=%async_computation | async-start | bytes 24576 | tf_op jit(solution)/shard_map/all_to_all | solution.py:99
  32.9 76.2 %all-to-all-start.1 = ((bf16[8,768,256]{2,1,0:T(8,128)(2,1)}), bf16[8,768,256]{2,1,0:T(8,128)(2,1)}, u32[]{:S(2)}, u32[]{:S(2)}) async-start(bf16[8,768,256]{2,1,0:T(8,128)(2,1)} %fusion.21), calls=%async_computation.1 | async-start | bytes 6291456 | tf_op jit(solution)/shard_map/all_to_all | solution.py:98
  38.9 101.2 %reduce-scatter.2.cloned.1.call-start = ((), (), s32[]{:S(2)}) async-start(), calls=%async_computation.4 | async-start | bytes 1310720 | tf_op jit(solution)/shard_map/reduce_scatter | solution.py:113
  109.2 6.0 %copy-start.2 = (bf16[1,1024]{1,0:T(2,128)(2,1)S(1)}, bf16[1,1024]{1,0:T(2,128)(2,1)}, u32[]{:S(2)}) copy-start(bf16[1,1024]{1,0:T(2,128)(2,1)} %param.8) | copy-start | bytes 6148
  115.2 10.1 %copy-start.1 = (bf16[1,256,4096]{2,1,0:T(8,128)(2,1)S(1)}, bf16[1,256,4096]{2,1,0:T(8,128)(2,1)}, u32[]{:S(2)}) copy-start(bf16[1,256,4096]{2,1,0:T(8,128)(2,1)} %param.6) | copy-start | bytes 6291460
  121.6 10.2 %all-to-all-start.2 = ((bf16[8,2,384]{2,1,0:T(2,128)(2,1)}), bf16[8,2,384]{2,1,0:T(2,128)(2,1)S(1)}, u32[]{:S(2)}, u32[]{:S(2)}) async-start(bf16[8,2,384]{2,1,0:T(2,128)(2,1)} %reshape.124), calls=%async_computation.3 | async-start | bytes 24576 | tf_op jit(solution)/shard_map/all_to_all | solution.py:100
Sparse Core Ops, SparseCore 0:
  115.3 23.9 reduce-scatter.1
where the time goes:
time: 159 us; the launch traced here: 158 us
  waiting for transfers between devices  76.2 us (48%)
  matrix products  34.5 us (22%)
  starting transfers between devices  17.1 us (11%)
  between operations  14.4 us (9%)
  other arithmetic  7.63 us (5%)
  blocking collectives  5.64 us (4%)
  local copies, waits for them, and re-layouts  2.9 us (2%)
    all_to_all x1, waiting for transfers between devices, body(): lax.all_to_all(send_rows, 'region', split_axis=0, concat_axis=0, tiled=True)  70 us
    all_to_all x1, starting transfers between devices, body(): lax.all_to_all(send_gain, 'region', split_axis=0, concat_axis=0, tiled=True)  7.25 us
    dot_general x1, matrix products, body(): jnp.einsum('rso,om->rsm', placement.astype(jnp.bfloat16), obs_anomaly[0],...  6.69 us
    all_to_all x1, waiting for transfers between devices, body(): lax.all_to_all(send_innov, 'region', split_axis=0, concat_axis=0, tiled=T...  6.17 us
    all_to_all x1, starting transfers between devices, body(): lax.all_to_all(send_rows, 'region', split_axis=0, concat_axis=0, tiled=True)  5.98 us
    psum x1, blocking collectives, body(): all_sums = lax.psum(sum_terms, 'level')  5.64 us
    dot_general x1, matrix products, body(): jnp.einsum('rso,or->rs', place_float, gain.astype(jnp.float32), precision...  5.22 us
    dot_general x1, matrix products, body(): jnp.einsum('rso,o->rs', place_float, innovation[0].astype(jnp.float32), p...  5.21 us
  transfers between devices with their start and end apart: 4, of which 2 were waited for; matrix products, arithmetic and copies ran while one was open for 10% of the time, Pallas kernels for 0%

commit v1 on v0

v1 whole, which is shorter than its diff:
```python
import functools
import math

import jax
import jax.numpy as jnp
from jax import lax
from jax.experimental import pallas as pl
from jax.experimental.pallas import tpu as pltpu
from jax.sharding import PartitionSpec as P

NSTEPS = 4
TAPER = 0.6
EXTRA = 16
F32 = jnp.float32
BF16 = jnp.bfloat16
MESH = pl.DeviceIdType.MESH


def each(count, step):
    if count <= 8:
        for k in range(count):
            step(k)
    else:
        lax.fori_loop(0, count, lambda k, c: (step(k), c)[1], 0)


def split(a):
    high = a.astype(BF16)
    return high, (a - high.astype(F32)).astype(BF16)


def dot(a, b):
    return jnp.dot(a, b, preferred_element_type=F32)


def product(a, b):
    return dot(a[0], b[0]) + (dot(a[0], b[1]) + dot(a[1], b[0]))


def weights_kernel(
    regions,
    levels,
    x_ref,
    owner_ref,
    prec_ref,
    innov_ref,
    neigh_ref,
    out_ref,
    gain,
    sums,
    xt,
    tx1,
    keep,
    rx1,
    tx2,
    rx2,
    tx3,
    rx3,
    mat,
    send1,
    recv1,
    send2,
    recv2,
    send3,
    recv3,
):
    groups = regions // 2
    members = x_ref.shape[1]
    half = members // 2
    me_r = lax.axis_index("region")
    me_l = lax.axis_index("level")
    my_group, side = lax.div(me_r, 2), lax.rem(me_r, 2)
    partner = my_group * 2 + (1 - side)

    def other_group(k):
        return lax.rem(my_group + 1 + k, groups)

    def other_level(k):
        return lax.rem(me_l + 1 + k, levels)

    barrier = pltpu.get_barrier_semaphore()

    def greet(region, level):
        pl.semaphore_signal(barrier, inc=1, device_id=(region, level), device_id_type=MESH)

    greet(partner, me_l)
    each(groups - 1, lambda k: greet(other_group(k) * 2 + side, me_l))
    each(levels - 1, lambda k: greet(me_r, other_level(k)))

    owner = owner_ref[...]
    ids = lax.broadcasted_iota(jnp.int32, (regions, owner.shape[1]), 0)
    weight = (ids == owner).astype(F32)
    for listed in range(neigh_ref.shape[1]):
        hit = (neigh_ref[:, listed : listed + 1] == owner).astype(F32)
        weight = weight + TAPER ** (listed + 1) * hit
    rounded = (weight * prec_ref[...].astype(F32)).astype(BF16).astype(F32)
    gain[...] = rounded
    sums[...] = dot((rounded * innov_ref[...].astype(F32)).astype(BF16), x_ref[...])
    xt[...] = x_ref[...].astype(F32).T

    row = lax.broadcasted_iota(jnp.int32, (half, half), 0)
    col = lax.broadcasted_iota(jnp.int32, (half, half), 1)
    line = lax.broadcasted_iota(jnp.int32, (EXTRA, half), 0)

    def contribution(region):
        weighted = (xt[...] * gain[pl.ds(region, 1), :]).astype(BF16)
        cov = dot(weighted, x_ref[...])
        low = cov[half:, half:]
        tri = jnp.where(row <= col, cov[:half, :half], low)
        diag = jnp.sum(jnp.where(row == col, low, 0.0), axis=0, keepdims=True)
        vec = sums[pl.ds(region, 1), :]
        extra = jnp.where(
            line == 0,
            diag,
            jnp.where(line == 1, vec[:, :half], jnp.where(line == 2, vec[:, half:], 0.0)),
        )
        return cov[:half, half:], tri, extra

    def store(ref, group, parts):
        kind = ref.dtype
        ref[group, 0:half, :] = parts[0].astype(kind)
        ref[group, half:members, :] = parts[1].astype(kind)
        ref[group, members : members + EXTRA, :] = parts[2].astype(kind)

    def copy1(group):
        return pltpu.make_async_remote_copy(
            src_ref=tx1.at[group],
            dst_ref=rx1.at[group],
            send_sem=send1.at[group],
            recv_sem=recv1.at[group],
            device_id=(partner, me_l),
            device_id_type=MESH,
        )

    def copy2(to, slot):
        return pltpu.make_async_remote_copy(
            src_ref=tx2.at[to],
            dst_ref=rx2.at[slot],
            send_sem=send2.at[to],
            recv_sem=recv2.at[slot],
            device_id=(to * 2 + side, me_l),
            device_id_type=MESH,
        )

    def copy3(to, slot):
        return pltpu.make_async_remote_copy(
            src_ref=tx3,
            dst_ref=rx3.at[slot],
            send_sem=send3.at[to],
            recv_sem=recv3.at[slot],
            device_id=(me_r, to),
            device_id_type=MESH,
        )

    store(tx1, other_group(0), contribution(other_group(0) * 2 + (1 - side)))
    pl.semaphore_wait(barrier, 1 + (groups - 1) + (levels - 1))
    copy1(other_group(0)).start()

    def give(k):
        group = other_group(k + 1)
        store(tx1, group, contribution(group * 2 + (1 - side)))
        copy1(group).start()

    each(groups - 1, give)

    def hold(k):
        group = other_group(k)
        store(keep, group, contribution(group * 2 + side))

    each(groups, hold)

    def fold(k):
        group = other_group(k)
        copy1(group).wait_recv()
        tx2[group] = (keep[group] + rx1[group].astype(F32)).astype(BF16)
        copy2(group, my_group).start()

    each(groups - 1, fold)
    copy1(my_group).wait_recv()
    keep[my_group] = keep[my_group] + rx1[my_group].astype(F32)

    def gather(k):
        group = other_group(k)
        copy2(group, group).wait_recv()
        keep[my_group] = keep[my_group] + rx2[group].astype(F32)

    each(groups - 1, gather)
    total = keep[my_group]
    tx3[...] = total.astype(BF16)
    each(levels - 1, lambda k: copy3(other_level(k), me_l).start())
    for k in range(levels - 1):
        level = other_level(k)
        apart = jnp.abs(level - me_l)
        factor = jnp.float32(0.0)
        for distance in range(1, levels):
            factor = jnp.where(apart == distance, jnp.float32(0.5**distance), factor)
        copy3(level, level).wait_recv()
        total = total + factor * rx3[level].astype(F32)

    corner = total[:half]
    tri = total[half:members]
    flip = tri.T
    shift = members - 1.0
    mat[0:half, half:members] = corner
    mat[half:members, 0:half] = corner.T
    mat[0:half, 0:half] = jnp.where(row <= col, tri, flip) + jnp.where(row == col, shift, 0.0)
    mat[half:members, half:members] = jnp.where(
        row == col,
        total[members : members + 1] + shift,
        jnp.where(row > col, tri, flip),
    )
    vector = jnp.concatenate(
        [total[members + 1 : members + 2], total[members + 2 : members + 3]], axis=1
    )
    matrix = mat[...]
    norm = 0.5 * jnp.sqrt(
        jnp.sum(jnp.sum(matrix * matrix, axis=0, keepdims=True), axis=1, keepdims=True)
    )
    eye = (
        lax.broadcasted_iota(jnp.int32, (members, members), 0)
        == lax.broadcasted_iota(jnp.int32, (members, members), 1)
    ).astype(F32)
    root_iter = matrix / norm
    correction = 1.5 * eye - 0.5 * root_iter
    inverse_iter = correction
    left, right = split(root_iter), split(correction)
    root_iter = product(left, right)
    inverse = right
    for step in range(1, NSTEPS):
        left = split(root_iter)
        correction = split(1.5 * eye - 0.5 * product(inverse, left))
        if step < NSTEPS - 1:
            root_iter = product(left, correction)
        inverse_iter = product(correction, inverse)
        inverse = split(inverse_iter)
    inner = product(split(jnp.broadcast_to(vector, (8, members))), inverse)
    mean_shift = product(split(inner), inverse)[0:1] / norm
    table = math.sqrt(members - 1.0) * (inverse_iter / jnp.sqrt(norm)) + mean_shift
    spare = (1.0 - jnp.sum(table, axis=1, keepdims=True)) * (1.0 / members)
    out_ref[...] = (table + spare).astype(BF16)

    each(groups, lambda k: copy1(other_group(k)).wait_send())
    each(groups - 1, lambda k: copy2(other_group(k), my_group).wait_send())
    each(levels - 1, lambda k: copy3(other_level(k), me_l).wait_send())


def update_kernel(table_ref, block_ref, out_ref):
    out_ref[...] = dot(table_ref[...], block_ref[...]).astype(BF16)


def body(ensemble, obs_anomaly, innovation, obs_precision, owner_region, neighbours):
    regions = lax.axis_size("region")
    levels = lax.axis_size("level")
    groups = regions // 2
    obs, members = obs_anomaly.shape[1:]
    rows, half = members + EXTRA, members // 2
    vmem = pl.BlockSpec(memory_space=pltpu.VMEM)
    dma = pltpu.SemaphoreType.DMA
    table = pl.pallas_call(
        functools.partial(weights_kernel, regions, levels),
        out_shape=jax.ShapeDtypeStruct((members, members), BF16),
        in_specs=[vmem] * 5,
        out_specs=vmem,
        scratch_shapes=[
            pltpu.VMEM((regions, obs), F32),
            pltpu.VMEM((regions, members), F32),
            pltpu.VMEM((members, obs), F32),
            pltpu.VMEM((groups, rows, half), BF16),
            pltpu.VMEM((groups, rows, half), F32),
            pltpu.VMEM((groups, rows, half), BF16),
            pltpu.VMEM((groups, rows, half), BF16),
            pltpu.VMEM((groups, rows, half), BF16),
            pltpu.VMEM((rows, half), BF16),
            pltpu.VMEM((levels, rows, half), BF16),
            pltpu.VMEM((members, members), F32),
            dma((groups,)),
            dma((groups,)),
            dma((groups,)),
            dma((groups,)),
            dma((levels,)),
            dma((levels,)),
        ],
        compiler_params=pltpu.CompilerParams(
            collective_id=0, has_side_effects=True, vmem_limit_bytes=36 * 2**20
        ),
    )(
        obs_anomaly[0],
        owner_region.reshape(1, obs),
        obs_precision,
        innovation,
        neighbours,
    )
    columns = ensemble.shape[2]
    width = 1024
    return pl.pallas_call(
        update_kernel,
        out_shape=jax.ShapeDtypeStruct(ensemble.shape, BF16),
        grid=(columns // width,),
        in_specs=[
            pl.BlockSpec((members, members), lambda i: (0, 0)),
            pl.BlockSpec((None, members, width), lambda i: (0, 0, i)),
        ],
        out_specs=pl.BlockSpec((None, members, width), lambda i: (0, 0, i)),
    )(table, ensemble)


def solution(mesh):
    return jax.shard_map(
        body,
        mesh=mesh,
        in_specs=(
            P("level", None, "region"),
            P("level", "region", None),
            P("level", "region"),
            P("level", "region"),
            P("level", "region", None),
            P(),
        ),
        out_specs=P("level", None, "region"),
        check_vma=False,
    )
```

time: 159 us -> 31.9 us (0.20)
  waiting for transfers between devices: 76.2 us -> 0 us
  matrix products: 34.5 us -> 0 us
  Pallas kernels: 0 us -> 26.9 us
  starting transfers between devices: 17.1 us -> 0 us
  between operations: 14.4 us -> 0.02 us
  other arithmetic: 7.63 us -> 0 us
  blocking collectives: 5.64 us -> 0 us
  local copies, waits for them, and re-layouts: 2.9 us -> 4.5 us
    all_to_all x3 -> x0, waiting for transfers between devices: 76.1 us -> none  [the longest x1 70 us: body(): lax.all_to_all(send_rows, 'region', split_axis=0, concat_axis=0, tiled=True)]
    dot_general x20 -> x0, matrix products: 34.5 us -> none  [the longest x1 6.69 us: body(): jnp.einsum('rso,om->rsm', placement.astype(jnp.bfloat16), obs_anomaly[0],...]
    pallas_call x0 -> x2, Pallas kernels: none -> 26.9 us  [the longest x1 22.6 us: body(): pl.pallas_call(functools.partial(weights_kernel, regions, levels), out_sh...]
    all_to_all x3 -> x0, starting transfers between devices: 16.9 us -> none  [the longest x1 7.25 us: body(): lax.all_to_all(send_gain, 'region', split_axis=0, concat_axis=0, tiled=True)]
    psum x1 -> x0, blocking collectives: 5.64 us -> none  [body(): all_sums = lax.psum(sum_terms, 'level')]
    unnamed x12 -> x11, local copies, waits for them, and re-layouts: 1.28 us -> 4.5 us
    another operation x3 -> x0, other arithmetic: 2.45 us -> none
    reduce_sum x2 -> x0, other arithmetic: 1.97 us -> none  [the longest x1 1.63 us: inverse_root(): norm_scale = 0.5 * jnp.sqrt(jnp.sum(matrix * matrix))]
  transfers between devices with their start and end apart: 4 -> 0, of which waited for: 2 -> 0; matrix products, arithmetic and copies ran while one was open for 10% -> 0% of each run, Pallas kernels for 0% -> 0%
where the time goes in v1:
time: 31.9 us; the launch traced here: 31.4 us
  Pallas kernels  26.9 us (84%)
  local copies, waits for them, and re-layouts  4.5 us (14%)
    pallas_call x1, Pallas kernels, body(): pl.pallas_call(functools.partial(weights_kernel, regions, levels), out_sh...  22.6 us
    unnamed x11, local copies, waits for them, and re-layouts  4.5 us
    pallas_call x1, Pallas kernels, body(): pl.pallas_call(update_kernel, out_shape=jax.ShapeDtypeStruct(ensemble.sha...  4.34 us

profile of v1, /device:TPU:0, one launch (start us, length us, event | category | flops | bytes accessed | tf_op | source)
XLA Modules:
  0.0 31.4 jit_solution(8749417309966212722)
XLA Ops:
  0.0 0.8 %copy.7.neigh_ref = s32[8,3]{1,0:T(8,128)S(1)} copy(s32[8,3]{0,1:T(4,128)} %param.11) | data formatting | bytes 192 | tf_op args[5]
  0.8 0.0 copy-start
  0.8 1.0 %copy-done = bf16[1,1024,256]{2,1,0:T(8,128)(2,1)S(1)} copy-done((bf16[1,1024,256]{2,1,0:T(8,128)(2,1)S(1)}, bf16[1,1024,256]{2,1,0:T(8,128)(2,1)}, u32[]{:S(2)}) %copy-start) | copy-done | bytes 524312
  1.8 0.0 copy-start.2
  1.8 0.7 %copy-done.2 = s32[1,1024,1]{1,2,0:T(1,128)S(1)} copy-done((s32[1,1024,1]{1,2,0:T(1,128)S(1)}, s32[1,1024,1]{1,2,0:T(1,128)}, u32[]{:S(2)}) %copy-start.2) | copy-done | bytes 4120
  2.5 0.0 copy-start.3
  2.5 0.7 %copy-done.3 = bf16[1,1024]{1,0:T(2,128)(2,1)S(1)} copy-done((bf16[1,1024]{1,0:T(2,128)(2,1)S(1)}, bf16[1,1024]{1,0:T(2,128)(2,1)}, u32[]{:S(2)}) %copy-start.3) | copy-done | bytes 2072
  3.2 0.0 copy-start.4
  3.2 0.7 %copy-done.4 = bf16[1,1024]{1,0:T(2,128)(2,1)S(1)} copy-done((bf16[1,1024]{1,0:T(2,128)(2,1)S(1)}, bf16[1,1024]{1,0:T(2,128)(2,1)}, u32[]{:S(2)}) %copy-start.4) | copy-done | bytes 2072
  3.9 22.6 %shard_map.64.table_ref = bf16[256,256]{1,0:T(8,128)(2,1)S(1)} custom-call(bf16[1024,256]{1,0:T(8,128)(2,1)S(1)} %bitcast.2, s32[1,1024]{1,0:T(1,128)S(1)} %bitcast.3, bf16[1,1024]{1,0:T(2,128)(2,1)S(1)} %copy-done.3, bf16[1,1024]{1,0:T(2,128)(2,1)S(1)} %copy-done.4, s32[8,3]{1,0:T(8,128)S(1)} %copy.7.neigh_ref), custom_call_target="tpu_custom_call" | custom-call | tf_op jit(solution)/shard_map/pallas_call | solution.py:259
  26.4 0.0 copy-start.1
  26.4 0.6 %copy-done.1 = bf16[256,256]{1,0:T(8,128)(2,1)} copy-done((bf16[256,256]{1,0:T(8,128)(2,1)}, bf16[256,256]{1,0:T(8,128)(2,1)S(1)}, u32[]{:S(2)}) %copy-start.1) | copy-done | bytes 131096
  27.1 4.3 %shard_map.65 = bf16[1,256,4096]{2,1,0:T(8,128)(2,1)} custom-call(bf16[256,256]{1,0:T(8,128)(2,1)} %copy-done.1, bf16[1,256,4096]{2,1,0:T(8,128)(2,1)} %block_ref.1), custom_call_target="tpu_custom_call" | custom-call | tf_op jit(solution)/shard_map/pallas_call | solution.py:295
Async XLA Ops:
  0.8 1.0 %copy-start = (bf16[1,1024,256]{2,1,0:T(8,128)(2,1)S(1)}, bf16[1,1024,256]{2,1,0:T(8,128)(2,1)}, u32[]{:S(2)}) copy-start(bf16[1,1024,256]{2,1,0:T(8,128)(2,1)} %param.7) | copy-start | bytes 1572868
  1.8 0.7 %copy-start.2 = (s32[1,1024,1]{1,2,0:T(1,128)S(1)}, s32[1,1024,1]{1,2,0:T(1,128)}, u32[]{:S(2)}) copy-start(s32[1,1024,1]{1,2,0:T(1,128)} %param.10) | copy-start | bytes 12292
  2.5 0.7 %copy-start.3 = (bf16[1,1024]{1,0:T(2,128)(2,1)S(1)}, bf16[1,1024]{1,0:T(2,128)(2,1)}, u32[]{:S(2)}) copy-start(bf16[1,1024]{1,0:T(2,128)(2,1)} %prec_ref.1) | copy-start | bytes 6148
  3.2 0.7 %copy-start.4 = (bf16[1,1024]{1,0:T(2,128)(2,1)S(1)}, bf16[1,1024]{1,0:T(2,128)(2,1)}, u32[]{:S(2)}) copy-start(bf16[1,1024]{1,0:T(2,128)(2,1)} %innov_ref.1) | copy-start | bytes 6148
  26.4 0.7 %copy-start.1 = (bf16[256,256]{1,0:T(8,128)(2,1)}, bf16[256,256]{1,0:T(8,128)(2,1)S(1)}, u32[]{:S(2)}) copy-start(bf16[256,256]{1,0:T(8,128)(2,1)S(1)} %shard_map.64.table_ref) | copy-start | bytes 393220

commit v2 on v1

--- a/solution.py
+++ b/solution.py
@@ -24,28 +24,44 @@
         lax.fori_loop(0, count, lambda k, c: (step(k), c)[1], 0)
 
 
-def split(a):
-    high = a.astype(BF16)
-    return high, (a - high.astype(F32)).astype(BF16)
-
-
 def dot(a, b):
     return jnp.dot(a, b, preferred_element_type=F32)
 
 
+def shifted(scale, rest):
+    return scale, rest, rest.astype(BF16)
+
+
 def product(a, b):
-    return dot(a[0], b[0]) + (dot(a[0], b[1]) + dot(a[1], b[0]))
+    return shifted(a[0] * b[0], a[0] * b[1] + b[0] * a[1] + dot(a[2], b[2]))
+
+
+def correct(a):
+    return shifted(1.5 - 0.5 * a[0], -0.5 * a[1])
+
+
+def apply(a, vector):
+    rows = jnp.broadcast_to(vector, (8, vector.shape[1]))
+    high = rows.astype(BF16)
+    low = (rows - high.astype(F32)).astype(BF16)
+    return (a[0] * rows + (dot(high, a[2]) + dot(low, a[2])))[0:1]
 
 
 def weights_kernel(
     regions,
     levels,
+    x_hbm,
+    owner_hbm,
+    prec_hbm,
+    innov_hbm,
+    neigh_hbm,
+    out_ref,
     x_ref,
     owner_ref,
     prec_ref,
     innov_ref,
     neigh_ref,
-    out_ref,
+    load_sem,
     gain,
     sums,
     xt,
@@ -78,6 +94,21 @@
     def other_level(k):
         return lax.rem(me_l + 1 + k, levels)
 
+    loads = [
+        pltpu.make_async_copy(source, target, load_sem.at[n])
+        for n, (source, target) in enumerate(
+            (
+                (neigh_hbm, neigh_ref),
+                (owner_hbm, owner_ref),
+                (prec_hbm, prec_ref),
+                (innov_hbm, innov_ref),
+                (x_hbm, x_ref),
+            )
+        )
+    ]
+    for load in loads:
+        load.start()
+
     barrier = pltpu.get_barrier_semaphore()
 
     def greet(region, level):
@@ -87,14 +118,27 @@
     each(groups - 1, lambda k: greet(other_group(k) * 2 + side, me_l))
     each(levels - 1, lambda k: greet(me_r, other_level(k)))
 
+    for load in loads[:4]:
+        load.wait()
     owner = owner_ref[...]
+    unit = (
+        lax.broadcasted_iota(jnp.int32, (regions, regions), 0)
+        == lax.broadcasted_iota(jnp.int32, (regions, regions), 1)
+    ).astype(F32)
+    lists = lax.dot_general(
+        unit.astype(BF16),
+        neigh_ref[...].astype(F32).astype(BF16),
+        (((1,), (1,)), ((), ())),
+        preferred_element_type=F32,
+    ).astype(jnp.int32)
     ids = lax.broadcasted_iota(jnp.int32, (regions, owner.shape[1]), 0)
     weight = (ids == owner).astype(F32)
-    for listed in range(neigh_ref.shape[1]):
-        hit = (neigh_ref[:, listed : listed + 1] == owner).astype(F32)
+    for listed in range(neigh_ref.shape[0]):
+        hit = (lists[:, listed : listed + 1] == owner).astype(F32)
         weight = weight + TAPER ** (listed + 1) * hit
     rounded = (weight * prec_ref[...].astype(F32)).astype(BF16).astype(F32)
     gain[...] = rounded
+    loads[4].wait()
     sums[...] = dot((rounded * innov_ref[...].astype(F32)).astype(BF16), x_ref[...])
     xt[...] = x_ref[...].astype(F32).T
 
@@ -220,32 +264,26 @@
         lax.broadcasted_iota(jnp.int32, (members, members), 0)
         == lax.broadcasted_iota(jnp.int32, (members, members), 1)
     ).astype(F32)
-    root_iter = matrix / norm
-    correction = 1.5 * eye - 0.5 * root_iter
-    inverse_iter = correction
-    left, right = split(root_iter), split(correction)
-    root_iter = product(left, right)
-    inverse = right
+    middle = jnp.sum(
+        jnp.sum(matrix * eye, axis=0, keepdims=True), axis=1, keepdims=True
+    ) / (members * norm)
+    root_iter = shifted(middle, matrix / norm - middle * eye)
+    inverse_iter = correct(root_iter)
+    root_iter = product(root_iter, inverse_iter)
     for step in range(1, NSTEPS):
-        left = split(root_iter)
-        correction = split(1.5 * eye - 0.5 * product(inverse, left))
+        correction = correct(product(inverse_iter, root_iter))
         if step < NSTEPS - 1:
-            root_iter = product(left, correction)
-        inverse_iter = product(correction, inverse)
-        inverse = split(inverse_iter)
-    inner = product(split(jnp.broadcast_to(vector, (8, members))), inverse)
-    mean_shift = product(split(inner), inverse)[0:1] / norm
-    table = math.sqrt(members - 1.0) * (inverse_iter / jnp.sqrt(norm)) + mean_shift
+            root_iter = product(root_iter, correction)
+        inverse_iter = product(correction, inverse_iter)
+    mean_shift = apply(inverse_iter, apply(inverse_iter, vector)) / norm
+    scale = math.sqrt(members - 1.0) * lax.rsqrt(norm)
+    table = scale * (inverse_iter[0] * eye + inverse_iter[1]) + mean_shift
     spare = (1.0 - jnp.sum(table, axis=1, keepdims=True)) * (1.0 / members)
     out_ref[...] = (table + spare).astype(BF16)
 
     each(groups, lambda k: copy1(other_group(k)).wait_send())
     each(groups - 1, lambda k: copy2(other_group(k), my_group).wait_send())
     each(levels - 1, lambda k: copy3(other_level(k), me_l).wait_send())
-
-
-def update_kernel(table_ref, block_ref, out_ref):
-    out_ref[...] = dot(table_ref[...], block_ref[...]).astype(BF16)
 
 
 def body(ensemble, obs_anomaly, innovation, obs_precision, owner_region, neighbours):
@@ -255,13 +293,20 @@
     obs, members = obs_anomaly.shape[1:]
     rows, half = members + EXTRA, members // 2
     vmem = pl.BlockSpec(memory_space=pltpu.VMEM)
+    hbm = pl.BlockSpec(memory_space=pltpu.HBM)
     dma = pltpu.SemaphoreType.DMA
     table = pl.pallas_call(
         functools.partial(weights_kernel, regions, levels),
         out_shape=jax.ShapeDtypeStruct((members, members), BF16),
-        in_specs=[vmem] * 5,
+        in_specs=[hbm] * 5,
         out_specs=vmem,
         scratch_shapes=[
+            pltpu.VMEM((obs, members), BF16),
+            pltpu.VMEM((1, obs), jnp.int32),
+            pltpu.VMEM((1, obs), BF16),
+            pltpu.VMEM((1, obs), BF16),
+            pltpu.VMEM(neighbours.shape[::-1], jnp.int32),
+            dma((5,)),
             pltpu.VMEM((regions, obs), F32),
             pltpu.VMEM((regions, members), F32),
             pltpu.VMEM((members, obs), F32),
@@ -281,27 +326,16 @@
             dma((levels,)),
         ],
         compiler_params=pltpu.CompilerParams(
-            collective_id=0, has_side_effects=True, vmem_limit_bytes=36 * 2**20
+            collective_id=0, has_side_effects=True, vmem_limit_bytes=61 * 2**20
         ),
     )(
         obs_anomaly[0],
         owner_region.reshape(1, obs),
         obs_precision,
         innovation,
-        neighbours,
-    )
-    columns = ensemble.shape[2]
-    width = 1024
-    return pl.pallas_call(
-        update_kernel,
-        out_shape=jax.ShapeDtypeStruct(ensemble.shape, BF16),
-        grid=(columns // width,),
-        in_specs=[
-            pl.BlockSpec((members, members), lambda i: (0, 0)),
-            pl.BlockSpec((None, members, width), lambda i: (0, 0, i)),
-        ],
-        out_specs=pl.BlockSpec((None, members, width), lambda i: (0, 0, i)),
-    )(table, ensemble)
+        neighbours.T,
+    )
+    return dot(table, ensemble[0]).astype(BF16)[None]
 
 
 def solution(mesh):

time: 31.9 us -> 25.7 us (0.81)
  local copies, waits for them, and re-layouts: 4.5 us -> 0.01 us
  Pallas kernels: 26.9 us -> 22.5 us
  matrix products: 0 us -> 2.94 us
    unnamed x11 -> x2, local copies, waits for them, and re-layouts: 4.5 us -> 0.01 us
    pallas_call x1 -> x0, Pallas kernels: 4.34 us -> none  [body(): pl.pallas_call(update_kernel, out_shape=jax.ShapeDtypeStruct(ensemble.sha...]
    dot_general x0 -> x1, matrix products: none -> 2.94 us  [dot(): return jnp.dot(a, b, preferred_element_type=F32)]
where the time goes in v2:
time: 25.7 us; the launch traced here: 25.5 us
  Pallas kernels  22.5 us (88%)
  matrix products  2.94 us (11%)
    pallas_call x1, Pallas kernels, body(): pl.pallas_call(functools.partial(weights_kernel, regions, levels), out_sh...  22.5 us
    dot_general x1, matrix products, dot(): return jnp.dot(a, b, preferred_element_type=F32)  2.94 us

profile of v2, /device:TPU:0, one launch (start us, length us, event | category | flops | bytes accessed | tf_op | source)
XLA Modules:
  0.0 25.5 jit_solution(15862869049535761089)
XLA Ops:
  0.0 0.0 copy-start
  0.0 22.5 %shard_map.64 = bf16[256,256]{1,0:T(8,128)(2,1)} custom-call(bf16[1024,256]{1,0:T(8,128)(2,1)} %bitcast.9, s32[1,1024]{1,0:T(1,128)} %bitcast.10, bf16[1,1024]{1,0:T(2,128)(2,1)} %prec_hbm.1, bf16[1,1024]{1,0:T(2,128)(2,1)} %innov_hbm.1, s32[3,8]{1,0:T(4,128)} %bitcast.11), custom_call_target="tpu_custom_call" | custom-call | tf_op jit(solution)/shard_map/pallas_call | solution.py:298
  22.5 0.0 copy-done
  22.5 2.9 %fusion = bf16[1,256,4096]{2,1,0:T(8,128)(2,1)} fusion(bf16[256,256]{1,0:T(8,128)(2,1)} %shard_map.64, bf16[1,256,4096]{2,1,0:T(8,128)(2,1)S(1)} %copy-done), kind=kOutput, calls=%fused_computation.1 | convolution fusion | flops 537919488 | bytes 4325376 | tf_op jit(solution)/shard_map/dot_general | solution.py:28
Async XLA Ops:
  0.0 22.5 %copy-start = (bf16[1,256,4096]{2,1,0:T(8,128)(2,1)S(1)}, bf16[1,256,4096]{2,1,0:T(8,128)(2,1)}, u32[]{:S(2)}) copy-start(bf16[1,256,4096]{2,1,0:T(8,128)(2,1)} %param.6) | copy-start | bytes 6291460

commit v3 on v2

--- a/solution.py
+++ b/solution.py
@@ -166,95 +166,112 @@
         ref[group, half:members, :] = parts[1].astype(kind)
         ref[group, members : members + EXTRA, :] = parts[2].astype(kind)
 
-    def copy1(group):
+    spans = (pl.ds(0, half), pl.ds(half, half + EXTRA))
+
+    def copy1(group, part):
         return pltpu.make_async_remote_copy(
-            src_ref=tx1.at[group],
-            dst_ref=rx1.at[group],
-            send_sem=send1.at[group],
-            recv_sem=recv1.at[group],
+            src_ref=tx1.at[group, spans[part]],
+            dst_ref=rx1.at[group, spans[part]],
+            send_sem=send1.at[part, group],
+            recv_sem=recv1.at[part, group],
             device_id=(partner, me_l),
             device_id_type=MESH,
         )
 
-    def copy2(to, slot):
+    def copy2(to, slot, part):
         return pltpu.make_async_remote_copy(
-            src_ref=tx2.at[to],
-            dst_ref=rx2.at[slot],
-            send_sem=send2.at[to],
-            recv_sem=recv2.at[slot],
+            src_ref=tx2.at[to, spans[part]],
+            dst_ref=rx2.at[slot, spans[part]],
+            send_sem=send2.at[part, to],
+            recv_sem=recv2.at[part, slot],
             device_id=(to * 2 + side, me_l),
             device_id_type=MESH,
         )
 
-    def copy3(to, slot):
+    def copy3(to, slot, part):
         return pltpu.make_async_remote_copy(
-            src_ref=tx3,
-            dst_ref=rx3.at[slot],
-            send_sem=send3.at[to],
-            recv_sem=recv3.at[slot],
+            src_ref=tx3.at[spans[part]],
+            dst_ref=rx3.at[slot, spans[part]],
+            send_sem=send3.at[part, to],
+            recv_sem=recv3.at[part, slot],
             device_id=(me_r, to),
             device_id_type=MESH,
         )
 
+    def hold(group):
+        store(keep, group, contribution(group * 2 + side))
+
+    def fold(k, part):
+        group, span = other_group(k), spans[part]
+        copy1(group, part).wait_recv()
+        tx2[group, span] = (keep[group, span] + rx1[group, span].astype(F32)).astype(BF16)
+        copy2(group, my_group, part).start()
+
+    def gather(part):
+        span = spans[part]
+        copy1(my_group, part).wait_recv()
+        keep[my_group, span] = keep[my_group, span] + rx1[my_group, span].astype(F32)
+
+        def add(k):
+            group = other_group(k)
+            copy2(group, group, part).wait_recv()
+            keep[my_group, span] = keep[my_group, span] + rx2[group, span].astype(F32)
+
+        each(groups - 1, add)
+        tx3[span] = keep[my_group, span].astype(BF16)
+        each(levels - 1, lambda k: copy3(other_level(k), me_l, part).start())
+
+    def mix(part):
+        total = keep[my_group, spans[part]]
+        for k in range(levels - 1):
+            level = other_level(k)
+            apart = jnp.abs(level - me_l)
+            factor = jnp.float32(0.0)
+            for distance in range(1, levels):
+                factor = jnp.where(apart == distance, jnp.float32(0.5**distance), factor)
+            copy3(level, level, part).wait_recv()
+            total = total + factor * rx3[level, spans[part]].astype(F32)
+        return total
+
     store(tx1, other_group(0), contribution(other_group(0) * 2 + (1 - side)))
     pl.semaphore_wait(barrier, 1 + (groups - 1) + (levels - 1))
-    copy1(other_group(0)).start()
+    copy1(other_group(0), 0).start()
 
     def give(k):
         group = other_group(k + 1)
         store(tx1, group, contribution(group * 2 + (1 - side)))
-        copy1(group).start()
+        copy1(group, 0).start()
 
     each(groups - 1, give)
-
-    def hold(k):
-        group = other_group(k)
-        store(keep, group, contribution(group * 2 + side))
-
-    each(groups, hold)
-
-    def fold(k):
-        group = other_group(k)
-        copy1(group).wait_recv()
-        tx2[group] = (keep[group] + rx1[group].astype(F32)).astype(BF16)
-        copy2(group, my_group).start()
-
-    each(groups - 1, fold)
-    copy1(my_group).wait_recv()
-    keep[my_group] = keep[my_group] + rx1[my_group].astype(F32)
-
-    def gather(k):
-        group = other_group(k)
-        copy2(group, group).wait_recv()
-        keep[my_group] = keep[my_group] + rx2[group].astype(F32)
-
-    each(groups - 1, gather)
-    total = keep[my_group]
-    tx3[...] = total.astype(BF16)
-    each(levels - 1, lambda k: copy3(other_level(k), me_l).start())
-    for k in range(levels - 1):
-        level = other_level(k)
-        apart = jnp.abs(level - me_l)
-        factor = jnp.float32(0.0)
-        for distance in range(1, levels):
-            factor = jnp.where(apart == distance, jnp.float32(0.5**distance), factor)
-        copy3(level, level).wait_recv()
-        total = total + factor * rx3[level].astype(F32)
-
-    corner = total[:half]
-    tri = total[half:members]
-    flip = tri.T
+    each(groups, lambda k: copy1(other_group(k), 1).start())
+
+    def hold_fold(k):
+        hold(other_group(k))
+        fold(k, 0)
+
+    each(groups - 1, hold_fold)
+    hold(my_group)
+    ahead = (groups - 1) * 2 // 3
+    each(ahead, lambda k: fold(k, 1))
+    gather(0)
+    each(groups - 1 - ahead, lambda k: fold(k + ahead, 1))
+    gather(1)
+
+    corner = mix(0)
     shift = members - 1.0
     mat[0:half, half:members] = corner
     mat[half:members, 0:half] = corner.T
+    total = mix(1)
+    tri = total[:half]
+    flip = tri.T
     mat[0:half, 0:half] = jnp.where(row <= col, tri, flip) + jnp.where(row == col, shift, 0.0)
     mat[half:members, half:members] = jnp.where(
         row == col,
-        total[members : members + 1] + shift,
+        total[half : half + 1] + shift,
         jnp.where(row > col, tri, flip),
     )
     vector = jnp.concatenate(
-        [total[members + 1 : members + 2], total[members + 2 : members + 3]], axis=1
+        [total[half + 1 : half + 2], total[half + 2 : half + 3]], axis=1
     )
     matrix = mat[...]
     norm = 0.5 * jnp.sqrt(
@@ -271,19 +288,39 @@
     inverse_iter = correct(root_iter)
     root_iter = product(root_iter, inverse_iter)
     for step in range(1, NSTEPS):
+        if step == NSTEPS - 1:
+            vector = apply(inverse_iter, apply(inverse_iter, vector))
         correction = correct(product(inverse_iter, root_iter))
         if step < NSTEPS - 1:
             root_iter = product(root_iter, correction)
         inverse_iter = product(correction, inverse_iter)
-    mean_shift = apply(inverse_iter, apply(inverse_iter, vector)) / norm
+    mean_shift = apply(correction, apply(correction, vector)) / norm
     scale = math.sqrt(members - 1.0) * lax.rsqrt(norm)
     table = scale * (inverse_iter[0] * eye + inverse_iter[1]) + mean_shift
     spare = (1.0 - jnp.sum(table, axis=1, keepdims=True)) * (1.0 / members)
     out_ref[...] = (table + spare).astype(BF16)
 
-    each(groups, lambda k: copy1(other_group(k)).wait_send())
-    each(groups - 1, lambda k: copy2(other_group(k), my_group).wait_send())
-    each(levels - 1, lambda k: copy3(other_level(k), me_l).wait_send())
+    for part in range(2):
+        each(groups, lambda k: copy1(other_group(k), part).wait_send())
+        each(groups - 1, lambda k: copy2(other_group(k), my_group, part).wait_send())
+        each(levels - 1, lambda k: copy3(other_level(k), me_l, part).wait_send())
+
+
+def update_kernel(pieces, table_hbm, block_ref, out_hbm, table, held, load_sem, store_sem):
+    load = pltpu.make_async_copy(table_hbm, table, load_sem)
+    load.start()
+    load.wait()
+    width = block_ref.shape[2] // pieces
+    stores = []
+    for n in range(pieces):
+        columns = pl.ds(n * width, width)
+        held[:, columns] = dot(table[...], block_ref[0, :, columns]).astype(BF16)
+        stores.append(
+            pltpu.make_async_copy(held.at[:, columns], out_hbm.at[0, :, columns], store_sem.at[n])
+        )
+        stores[n].start()
+    for store in stores:
+        store.wait()
 
 
 def body(ensemble, obs_anomaly, innovation, obs_precision, owner_region, neighbours):
@@ -318,15 +355,20 @@
             pltpu.VMEM((rows, half), BF16),
             pltpu.VMEM((levels, rows, half), BF16),
             pltpu.VMEM((members, members), F32),
-            dma((groups,)),
-            dma((groups,)),
-            dma((groups,)),
-            dma((groups,)),
-            dma((levels,)),
-            dma((levels,)),
+            dma((2, groups)),
+            dma((2, groups)),
+            dma((2, groups)),
+            dma((2, groups)),
+            dma((2, levels)),
+            dma((2, levels)),
         ],
         compiler_params=pltpu.CompilerParams(
             collective_id=0, has_side_effects=True, vmem_limit_bytes=61 * 2**20
+        ),
+        cost_estimate=pl.CostEstimate(
+            flops=20 * obs * members * members * regions,
+            bytes_accessed=64 * obs * members,
+            transcendentals=0,
         ),
     )(
         obs_anomaly[0],
@@ -335,7 +377,20 @@
         innovation,
         neighbours.T,
     )
-    return dot(table, ensemble[0]).astype(BF16)[None]
+    pieces = 8
+    return pl.pallas_call(
+        functools.partial(update_kernel, pieces),
+        out_shape=jax.ShapeDtypeStruct(ensemble.shape, BF16),
+        in_specs=[hbm, vmem],
+        out_specs=hbm,
+        scratch_shapes=[
+            pltpu.VMEM((members, members), BF16),
+            pltpu.VMEM(ensemble.shape[1:], BF16),
+            dma(()),
+            dma((pieces,)),
+        ],
+        compiler_params=pltpu.CompilerParams(vmem_limit_bytes=16 * 2**20),
+    )(table, ensemble)
 
 
 def solution(mesh):

time: 25.7 us -> 25.5 us (level)
  matrix products: 2.94 us -> 0 us
  Pallas kernels: 22.5 us -> 24.4 us
  local copies, waits for them, and re-layouts: 0.01 us -> 0.9 us
    dot_general x1 -> x0, matrix products: 2.94 us -> none  [dot(): return jnp.dot(a, b, preferred_element_type=F32)]
    pallas_call x0 -> x1, Pallas kernels: none -> 1.75 us  [body(): pl.pallas_call(functools.partial(update_kernel, pieces), out_shape=jax.Sh...]
    unnamed x2 -> x4, local copies, waits for them, and re-layouts: 0.01 us -> 0.9 us
where the time goes in v3:
time: 25.5 us; the launch traced here: 25.3 us
  Pallas kernels  24.4 us (96%)
  local copies, waits for them, and re-layouts  0.9 us (4%)
    pallas_call x1, Pallas kernels, body(): pl.pallas_call(functools.partial(weights_kernel, regions, levels), out_sh...  22.6 us
    pallas_call x1, Pallas kernels, body(): pl.pallas_call(functools.partial(update_kernel, pieces), out_shape=jax.Sh...  1.75 us
    unnamed x4, local copies, waits for them, and re-layouts  0.9 us

profile of v3, /device:TPU:0, one launch (start us, length us, event | category | flops | bytes accessed | tf_op | source)
XLA Modules:
  0.0 25.3 jit_solution(5464461078003994434)
XLA Ops:
  0.0 0.0 copy-start
  0.0 22.6 %shard_map.64.table_hbm = bf16[256,256]{1,0:T(8,128)(2,1)} custom-call(bf16[1024,256]{1,0:T(8,128)(2,1)} %bitcast.3, s32[1,1024]{1,0:T(1,128)} %bitcast.4, bf16[1,1024]{1,0:T(2,128)(2,1)} %prec_hbm.1, bf16[1,1024]{1,0:T(2,128)(2,1)} %innov_hbm.1, s32[3,8]{1,0:T(4,128)} %bitcast.5), custom_call_target="tpu_custom_call" | custom-call | flops 10737418240 | bytes 16777216 | tf_op jit(solution)/shard_map/pallas_call | solution.py:335
  22.6 0.0 copy-done
  22.7 0.0 copy-start.1
  22.7 0.9 %copy-done.1 = bf16[256,256]{1,0:T(8,128)(2,1)S(1)} copy-done((bf16[256,256]{1,0:T(8,128)(2,1)S(1)}, bf16[256,256]{1,0:T(8,128)(2,1)}, u32[]{:S(2)}) %copy-start.1) | copy-done | bytes 131096
  23.6 1.8 %shard_map.65 = bf16[1,256,4096]{2,1,0:T(8,128)(2,1)} custom-call(bf16[256,256]{1,0:T(8,128)(2,1)S(1)} %copy-done.1, bf16[1,256,4096]{2,1,0:T(8,128)(2,1)S(1)} %copy-done), custom_call_target="tpu_custom_call" | custom-call | tf_op jit(solution)/shard_map/pallas_call | solution.py:381
Async XLA Ops:
  0.0 22.6 %copy-start = (bf16[1,256,4096]{2,1,0:T(8,128)(2,1)S(1)}, bf16[1,256,4096]{2,1,0:T(8,128)(2,1)}, u32[]{:S(2)}) copy-start(bf16[1,256,4096]{2,1,0:T(8,128)(2,1)} %block_ref.1) | copy-start | bytes 6291460
  22.7 0.9 %copy-start.1 = (bf16[256,256]{1,0:T(8,128)(2,1)S(1)}, bf16[256,256]{1,0:T(8,128)(2,1)}, u32[]{:S(2)}) copy-start(bf16[256,256]{1,0:T(8,128)(2,1)} %shard_map.64.table_hbm) | copy-start | bytes 393220

commit v4 on v3

--- a/solution.py
+++ b/solution.py
@@ -98,11 +98,11 @@
         pltpu.make_async_copy(source, target, load_sem.at[n])
         for n, (source, target) in enumerate(
             (
+                (x_hbm, x_ref),
                 (neigh_hbm, neigh_ref),
                 (owner_hbm, owner_ref),
                 (prec_hbm, prec_ref),
                 (innov_hbm, innov_ref),
-                (x_hbm, x_ref),
             )
         )
     ]
@@ -118,7 +118,7 @@
     each(groups - 1, lambda k: greet(other_group(k) * 2 + side, me_l))
     each(levels - 1, lambda k: greet(me_r, other_level(k)))
 
-    for load in loads[:4]:
+    for load in loads[1:]:
         load.wait()
     owner = owner_ref[...]
     unit = (
@@ -138,16 +138,16 @@
         weight = weight + TAPER ** (listed + 1) * hit
     rounded = (weight * prec_ref[...].astype(F32)).astype(BF16).astype(F32)
     gain[...] = rounded
-    loads[4].wait()
+    loads[0].wait()
     sums[...] = dot((rounded * innov_ref[...].astype(F32)).astype(BF16), x_ref[...])
-    xt[...] = x_ref[...].astype(F32).T
+    xt[...] = x_ref[...].T
 
     row = lax.broadcasted_iota(jnp.int32, (half, half), 0)
     col = lax.broadcasted_iota(jnp.int32, (half, half), 1)
     line = lax.broadcasted_iota(jnp.int32, (EXTRA, half), 0)
 
     def contribution(region):
-        weighted = (xt[...] * gain[pl.ds(region, 1), :]).astype(BF16)
+        weighted = xt[...] * gain[pl.ds(region, 1), :].astype(BF16)
         cov = dot(weighted, x_ref[...])
         low = cov[half:, half:]
         tri = jnp.where(row <= col, cov[:half, :half], low)
@@ -306,15 +306,25 @@
         each(levels - 1, lambda k: copy3(other_level(k), me_l, part).wait_send())
 
 
-def update_kernel(pieces, table_hbm, block_ref, out_hbm, table, held, load_sem, store_sem):
-    load = pltpu.make_async_copy(table_hbm, table, load_sem)
-    load.start()
-    load.wait()
-    width = block_ref.shape[2] // pieces
+def update_kernel(
+    pieces, table_hbm, block_hbm, out_hbm, table, block, held, table_sem, load_sem, store_sem
+):
+    width = block.shape[1] // pieces
+    first = pltpu.make_async_copy(table_hbm, table, table_sem)
+    first.start()
+    loads = []
+    for n in range(pieces):
+        columns = pl.ds(n * width, width)
+        loads.append(
+            pltpu.make_async_copy(block_hbm.at[0, :, columns], block.at[:, columns], load_sem.at[n])
+        )
+        loads[n].start()
+    first.wait()
     stores = []
     for n in range(pieces):
         columns = pl.ds(n * width, width)
-        held[:, columns] = dot(table[...], block_ref[0, :, columns]).astype(BF16)
+        loads[n].wait()
+        held[:, columns] = dot(table[...], block[:, columns]).astype(BF16)
         stores.append(
             pltpu.make_async_copy(held.at[:, columns], out_hbm.at[0, :, columns], store_sem.at[n])
         )
@@ -346,7 +356,7 @@
             dma((5,)),
             pltpu.VMEM((regions, obs), F32),
             pltpu.VMEM((regions, members), F32),
-            pltpu.VMEM((members, obs), F32),
+            pltpu.VMEM((members, obs), BF16),
             pltpu.VMEM((groups, rows, half), BF16),
             pltpu.VMEM((groups, rows, half), F32),
             pltpu.VMEM((groups, rows, half), BF16),
@@ -381,15 +391,17 @@
     return pl.pallas_call(
         functools.partial(update_kernel, pieces),
         out_shape=jax.ShapeDtypeStruct(ensemble.shape, BF16),
-        in_specs=[hbm, vmem],
+        in_specs=[hbm, hbm],
         out_specs=hbm,
         scratch_shapes=[
             pltpu.VMEM((members, members), BF16),
             pltpu.VMEM(ensemble.shape[1:], BF16),
+            pltpu.VMEM(ensemble.shape[1:], BF16),
             dma(()),
             dma((pieces,)),
+            dma((pieces,)),
         ],
-        compiler_params=pltpu.CompilerParams(vmem_limit_bytes=16 * 2**20),
+        compiler_params=pltpu.CompilerParams(vmem_limit_bytes=61 * 2**20),
     )(table, ensemble)
 
 

time: 25.5 us -> 26.9 us (1.055)
  Pallas kernels: 24.4 us -> 26.7 us
  local copies, waits for them, and re-layouts: 0.9 us -> 0 us
    pallas_call x1, Pallas kernels: 1.75 us -> 4.14 us  [body(): pl.pallas_call(functools.partial(update_kernel, pieces), out_shape=jax.Sh...]
    unnamed x4 -> x0, local copies, waits for them, and re-layouts: 0.9 us -> none
where the time goes in v4:
time: 26.9 us; the launch traced here: 26.7 us
  Pallas kernels  26.7 us (99%)
    pallas_call x1, Pallas kernels, body(): pl.pallas_call(functools.partial(weights_kernel, regions, levels), out_sh...  22.6 us
    pallas_call x1, Pallas kernels, body(): pl.pallas_call(functools.partial(update_kernel, pieces), out_shape=jax.Sh...  4.14 us

profile of v4, /device:TPU:0, one launch (start us, length us, event | category | flops | bytes accessed | tf_op | source)
XLA Modules:
  0.0 26.7 jit_solution(11556398712791287205)
XLA Ops:
  0.0 22.6 %shard_map.64.table_hbm = bf16[256,256]{1,0:T(8,128)(2,1)} custom-call(bf16[1024,256]{1,0:T(8,128)(2,1)} %bitcast.3, s32[1,1024]{1,0:T(1,128)} %bitcast.4, bf16[1,1024]{1,0:T(2,128)(2,1)} %prec_hbm.1, bf16[1,1024]{1,0:T(2,128)(2,1)} %innov_hbm.1, s32[3,8]{1,0:T(4,128)} %bitcast.5), custom_call_target="tpu_custom_call" | custom-call | flops 10737418240 | bytes 16777216 | tf_op jit(solution)/shard_map/pallas_call | solution.py:345
  22.6 4.1 %shard_map.65 = bf16[1,256,4096]{2,1,0:T(8,128)(2,1)} custom-call(bf16[256,256]{1,0:T(8,128)(2,1)} %shard_map.64.table_hbm, bf16[1,256,4096]{2,1,0:T(8,128)(2,1)} %block_hbm.1), custom_call_target="tpu_custom_call" | custom-call | tf_op jit(solution)/shard_map/pallas_call | solution.py:391
